TPU v7x, 32 devices: a whole 2x2x4 slice. The times are simulated.
32 devices in a mesh: img: 2 (over x), row: 4 (over z), col: 4 (over y, core).
Axes of the slice: x: 2, y: 2, z: 4, core: 2. Of those that a mesh axis runs over, the one named last changes fastest.
Arguments:
- latent: bfloat16 [128, 64, 1280], P(('img', 'row'), 'col'), parts along dimension 0, may hold values from -240 to 240
- norm_gain: float32 [1280], replicated, may hold values from 0.1 to 1.9
- norm_shift: float32 [1280], replicated, may hold values from -3 to 3
- query_weight: bfloat16 [1280, 768], replicated, may hold values from -0.25 to 0.25
- key_weight: bfloat16 [1280, 768], replicated, may hold values from -0.25 to 0.25
- value_weight: bfloat16 [1280, 768], replicated, may hold values from -0.15625 to 0.15625
- output_weight: bfloat16 [768, 1280], replicated, may hold values from -0.875 to 0.875
- output_bias: float32 [1280], replicated, may hold values from -3 to 3
Outputs:
- attended: bfloat16 [128, 64, 1280], P(('img', 'row'), 'col'), parts along dimension 0
There are 2 independent parts, one for each index of `img`. A program takes and returns all parts, laid end to end along the dimension named above; an argument that names none is the same for every part. Nothing has to cross between parts.
All inputs are finite; a program needn't handle non-finite values.
Results may differ from a plain program's by a relative error of at most 0.012.
The roundings to bfloat16 on the way count: a program that leaves them out, or rounds other values in their place, can miss the bound.
Values may be sent and summed in bfloat16 or wider, within the bound.
A program may use at most 128 MiB of HBM per device.

v0:
```python
import math

import jax
import jax.numpy as jnp
from jax import lax
from jax.sharding import PartitionSpec as P

GROUPS = 32
HD = 64


def attend(carry, piece, queries):
    keys, values = piece
    heads_here = queries.shape[1] // HD
    scale = 1.0 / math.sqrt(HD)
    query_heads = queries.reshape(queries.shape[0], heads_here, HD).transpose(1, 0, 2)
    key_heads = keys.reshape(keys.shape[0], heads_here, HD).transpose(1, 0, 2)
    value_heads = values.reshape(values.shape[0], heads_here, HD).transpose(1, 0, 2)

    def per_head(items):
        query_one, key_one, value_one, peak_old, total_old, mixed_old = items
        scores = jnp.dot(query_one, key_one.T, preferred_element_type=jnp.float32) * scale
        peak_new = jnp.maximum(peak_old, jnp.max(scores, axis=1))
        factor = jnp.exp(peak_old - peak_new)
        weights = jnp.exp(scores - peak_new[:, None])
        total_new = total_old * factor + jnp.sum(weights, axis=1)
        rounded = weights.astype(jnp.bfloat16)
        mixed_new = mixed_old * factor[:, None] + jnp.dot(
            rounded, value_one, preferred_element_type=jnp.float32
        )
        return (peak_new, total_new, mixed_new)

    return lax.map(per_head, (query_heads, key_heads, value_heads) + tuple(carry))


def start_state(queries):
    heads_here = queries.shape[1] // HD
    count = queries.shape[0]
    peak = jnp.full((heads_here, count), -1e30, jnp.float32)
    total = jnp.zeros((heads_here, count), jnp.float32)
    mixed = jnp.zeros((heads_here, count, HD), jnp.float32)
    return (peak, total, mixed)


def finish(state):
    peak, total, mixed = state
    heads_here, count, _ = mixed.shape
    result = mixed / total[:, :, None]
    return result.transpose(1, 0, 2).reshape(count, heads_here * HD).astype(jnp.bfloat16)


def local(
    latent,
    norm_gain,
    norm_shift,
    query_weight,
    key_weight,
    value_weight,
    output_weight,
    output_bias,
):
    rows_here, cols_here, width = latent.shape
    tok_count = rows_here * cols_here
    wide = latent.reshape(tok_count, width).astype(jnp.float32)
    grouped = wide.reshape(tok_count, GROUPS, width // GROUPS)
    entries = float(tok_count * lax.axis_size("row") * lax.axis_size("col") * (width // GROUPS))
    group_total = lax.psum(jnp.sum(grouped, axis=(0, 2)), ("row", "col"))
    mean = group_total / entries
    centered = grouped - mean[None, :, None]
    spread = lax.psum(jnp.sum(centered * centered, axis=(0, 2)), ("row", "col"))
    variance = spread / entries
    scaled = (centered * lax.rsqrt(variance + 1e-05)[None, :, None]).reshape(tok_count, width)
    normed = (scaled * norm_gain + norm_shift).astype(jnp.bfloat16)
    queries = jnp.dot(normed, query_weight, preferred_element_type=jnp.float32).astype(jnp.bfloat16)
    keys = jnp.dot(normed, key_weight, preferred_element_type=jnp.float32).astype(jnp.bfloat16)
    values = jnp.dot(normed, value_weight, preferred_element_type=jnp.float32).astype(jnp.bfloat16)
    state = attend(
        start_state(queries),
        (
            lax.all_gather(keys, ("row", "col"), axis=0, tiled=True),
            lax.all_gather(values, ("row", "col"), axis=0, tiled=True),
        ),
        queries,
    )
    mixed = finish(state)
    result = jnp.dot(mixed, output_weight, preferred_element_type=jnp.float32) + output_bias
    return result.astype(jnp.bfloat16).reshape(rows_here, cols_here, width)


def solution(mesh):
    placed = (P(("img", "row"), "col", None), P(), P(), P(), P(), P(), P(), P())
    return jax.shard_map(
        local, mesh=mesh, in_specs=placed, out_specs=P(("img", "row"), "col", None), check_vma=False
    )
```

profile of v0, /device:TPU:0, one launch (start us, length us, event | category | flops | bytes accessed | tf_op | source)
XLA Modules:
  0.0 272.7 jit_solution(14949438277409626070)
XLA Ops:
  6.5 1.3 convert_reduce_fusion
  7.9 0.1 reduce_sum.36
  8.0 0.1 reduce_sum.37
  8.1 34.9 %psum.14 = f32[32]{0:T(128)S(1)} all-reduce(f32[32]{0:T(128)S(1)} %reduce_sum.37), channel_id=1, replica_groups=mesh['img'=2,'row'=4,'col'=4] {'row','col'}, use_global_device_ids=true, to_apply=%region_2.0 | all-reduce | flops 32 | bytes 256 | tf_op jit(solution)/shard_map/psum | solution.py:67
  43.0 0.1 sub.41
  43.1 0.1 sub.42
  43.2 1.3 multiply_reduce_fusion
  44.5 0.1 reduce_sum.47
  44.5 0.1 reduce_sum.48
  44.7 29.5 %psum.15 = f32[32]{0:T(128)S(1)} all-reduce(f32[32]{0:T(128)S(1)} %reduce_sum.48), channel_id=1, replica_groups=mesh['img'=2,'row'=4,'col'=4] {'row','col'}, use_global_device_ids=true, to_apply=%region_5.6 | all-reduce | flops 32 | bytes 256 | tf_op jit(solution)/shard_map/psum | solution.py:70
  74.2 0.1 mul.49
  74.2 0.1 mul.50
  74.3 1.3 fusion.27
  75.7 0.0 copy-start.1
  75.7 3.2 %convolution_convert_fusion = bf16[256,768]{1,0:T(8,128)(2,1)} fusion(bf16[256,1280]{1,0:T(8,128)(2,1)S(1)} %fusion.27, bf16[1280,768]{1,0:T(8,128)(2,1)} %param.15), kind=kOutput, calls=%fused_computation.28 | convolution fusion | flops 503513088 | bytes 3014656 | tf_op jit(solution)/shard_map/dot_general | solution.py:76
  78.9 0.0 all-gather.5.cloned.1.call-update
  78.9 0.0 all-gather.3.cloned.1.call-start
  79.0 3.0 %convolution_convert_fusion.1 = bf16[256,768]{1,0:T(8,128)(2,1)} fusion(bf16[256,1280]{1,0:T(8,128)(2,1)S(1)} %fusion.27, bf16[1280,768]{1,0:T(8,128)(2,1)} %param.14), kind=kOutput, calls=%fused_computation.29 | convolution fusion | flops 503513088 | bytes 3014656 | tf_op jit(solution)/shard_map/dot_general | solution.py:75
  81.9 0.0 all-gather.3.cloned.1.call-update
  82.0 2.5 convolution_convert_fusion.2
  84.5 0.2 copy.18
  84.7 53.5 %all-gather.5.cloned.1.call-done = bf16[4096,768]{1,0:T(8,128)(2,1)} async-done(((bf16[256,768]{1,0:T(8,128)(2,1)}), bf16[4096,768]{1,0:T(8,128)(2,1)}) %all-gather.5.cloned.1.call-update) | async-done | bytes 6291472 | tf_op jit(solution)/shard_map/all_gather | solution.py:81
  138.2 8.8 %copy.20 = bf16[4096,768]{0,1:T(8,128)(2,1)} copy(bf16[4096,768]{1,0:T(8,128)(2,1)} %all-gather.5.cloned.1.call-done) | data formatting | bytes 12582912 | tf_op jit(solution)/shard_map/all_gather | solution.py:81
  146.9 54.0 %all-gather.3.cloned.1.call-done = bf16[4096,768]{1,0:T(8,128)(2,1)} async-done(((bf16[256,768]{1,0:T(8,128)(2,1)}), bf16[4096,768]{1,0:T(8,128)(2,1)}) %all-gather.3.cloned.1.call-update) | async-done | bytes 6291472 | tf_op jit(solution)/shard_map/all_gather | solution.py:80
  200.9 8.6 %copy.19 = bf16[4096,768]{0,1:T(8,128)(2,1)} copy(bf16[4096,768]{1,0:T(8,128)(2,1)} %all-gather.3.cloned.1.call-done) | data formatting | bytes 12582912 | tf_op jit(solution)/shard_map/all_gather | solution.py:80
  209.6 54.7 %while.12 = (s32[]{:T(128)}, f32[12,256]{1,0:T(8,128)S(1)}, f32[12,256,64]{1,2,0:T(8,128)S(1)}, bf16[12,256,64]{1,2,0:T(8,128)(2,1)S(1)}, bf16[12,4096,64]{1,2,0...) while((s32[]{:T(128)}, f32[12,256]{1,0:T(8,128)S(1)}, ...), condition=%wide.region_9.10_spmd, body=%wide.region_6.9_spmd.sunk | while | flops 274744064 | bytes 13745249 | solution.py:33
  209.6 1.9 fusion.44
  211.4 0.7 fusion.45
  212.2 1.9 fusion.46
  214.1 1.9 fusion.44
  216.0 0.7 fusion.45
  216.7 1.9 fusion.46
  218.7 1.9 fusion.44
  220.5 0.7 fusion.45
  221.3 1.9 fusion.46
  223.2 1.9 fusion.44
  225.1 0.7 fusion.45
  225.8 1.9 fusion.46
  227.8 1.9 fusion.44
  229.6 0.7 fusion.45
  230.4 1.9 fusion.46
  232.3 1.9 fusion.44
  234.2 0.7 fusion.45
  234.9 1.9 fusion.46
  236.9 1.9 fusion.44
  238.8 0.7 fusion.45
  239.5 1.9 fusion.46
  241.5 1.9 fusion.44
  243.3 0.7 fusion.45
  244.0 1.9 fusion.46
  246.0 1.9 fusion.44
  247.9 0.7 fusion.45
  248.6 1.9 fusion.46
  250.6 1.9 fusion.44
  252.4 0.7 fusion.45
  253.2 1.9 fusion.46
  255.1 1.9 fusion.44
  257.0 0.7 fusion.45
  257.7 1.9 fusion.46
  259.7 1.9 fusion.44
  261.5 0.7 fusion.45
  262.3 1.9 fusion.46
  264.2 0.1 divide_convert_fusion
  264.3 1.5 fusion.23
  (46 shorter events, 0.7 us)
Async XLA Ops:
  6.5 257.8 %copy-start = (bf16[768,1280]{1,0:T(8,128)(2,1)S(1)}, bf16[768,1280]{1,0:T(8,128)(2,1)}, u32[]{:S(2)}) copy-start(bf16[768,1280]{1,0:T(8,128)(2,1)} %param.16) | copy-start | bytes 5898244
  6.5 131.6 %all-gather.5.cloned.1.call-start = ((), (), s32[]{:S(2)}) async-start(), calls=%async_computation.1 | async-start | bytes 6684672 | tf_op jit(solution)/shard_map/all_gather | solution.py:81
  75.7 6.3 %copy-start.1 = (bf16[256,1280]{1,0:T(8,128)(2,1)}, bf16[256,1280]{1,0:T(8,128)(2,1)S(1)}, u32[]{:S(2)}) copy-start(bf16[256,1280]{1,0:T(8,128)(2,1)S(1)} %fusion.27) | copy-start | bytes 1966084
  78.9 122.0 %all-gather.3.cloned.1.call-start = ((), (), s32[]{:S(2)}) async-start(), calls=%async_computation | async-start | bytes 6684672 | tf_op jit(solution)/shard_map/all_gather | solution.py:80
  209.6 54.8 %copy-start.2 = (f32[1280]{0:T(1024)S(1)}, f32[1280]{0:T(1024)}, u32[]{:S(2)}) copy-start(f32[1280]{0:T(1024)} %param.17) | copy-start | bytes 15364
Sparse Core Ops, SparseCore 0:
  79.0 59.0 all-gather.4
  140.5 60.4 all-gather.2
where the time goes:
time: 275 us; the launch traced here: 273 us
  waiting for transfers between devices  108 us (39%)
  blocking collectives  64.4 us (23%)
  matrix products  55.3 us (20%)
  local copies, waits for them, and re-layouts  18.5 us (7%)
  between operations  13.5 us (5%)
  other arithmetic  13.1 us (5%)
    all_gather x1, waiting for transfers between devices, local(): lax.all_gather(keys, ('row', 'col'), axis=0, tiled=True)  54 us
    all_gather x1, waiting for transfers between devices, local(): lax.all_gather(values, ('row', 'col'), axis=0, tiled=True)  53.5 us
    psum x1, blocking collectives, local(): group_total = lax.psum(jnp.sum(grouped, axis=(0, 2)), ('row', 'col'))  34.9 us
    psum x1, blocking collectives, local(): spread = lax.psum(jnp.sum(centered * centered, axis=(0, 2)), ('row', 'col'))  29.5 us
    dot_general x12, matrix products, per_head(): jnp.dot(rounded, value_one, preferred_element_type=jnp.float32)  22.8 us
    dot_general x12, matrix products, per_head(): jnp.dot(query_one, key_one.T, preferred_element_type=jnp.float32) * scale  22.3 us
    all_gather x1, local copies, waits for them, and re-layouts, local(): lax.all_gather(values, ('row', 'col'), axis=0, tiled=True)  8.75 us
    all_gather x1, local copies, waits for them, and re-layouts, local(): lax.all_gather(keys, ('row', 'col'), axis=0, tiled=True)  8.61 us
  transfers between devices with their start and end apart: 2, of which 2 were waited for; matrix products, arithmetic and copies ran while one was open for 5% of the time, Pallas kernels for 0%

commit v1 on v0

v1 whole, which is shorter than its diff:
```python
import functools
import math

import jax
import jax.numpy as jnp
from jax import lax
from jax.experimental import pallas as pl
from jax.experimental.pallas import tpu as pltpu
from jax.sharding import PartitionSpec as P

GROUPS = 32
HD = 64
MESH = pl.DeviceIdType.MESH
F32 = jnp.float32
BF16 = jnp.bfloat16


def xor(a, s):
    out, bit = a, 1
    while bit <= s:
        if s & bit:
            out = out + bit * (1 - 2 * ((a // bit) % 2))
        bit *= 2
    return out


def xor_traced(a, s, n):
    out, bit = 0, 1
    while bit < n:
        out = out + bit * (((a // bit) + (s // bit)) % 2)
        bit *= 2
    return out


def kernel(
    ax_a, ax_b, na, nb, tok, width, wide_heads, per,
    x_hbm, gain_ref, shift_ref, wq_hbm, wk_hbm, wv_hbm, wo_hbm, bias_ref,
    out_ref,
    x_v, wq, wk, wv, wo, stat_own, stat_in, q_own, q_in, kv_own, kv, qh, m_s, acc, mix_out, mix_in,
    load_sem, own_sem, st_send, st_recv, q_send, q_recv, z_send, z_recv, f_send, f_recv, o_send, o_recv,
):
    me_a = lax.axis_index(ax_a)
    me_b = lax.axis_index(ax_b)
    gw = per * HD
    padw = kv.shape[-1]
    everyone = [(s, t) for s in range(na) for t in range(nb) if s or t]

    def dev(s, t):
        return {ax_a: xor(me_a, s), ax_b: xor(me_b, t)}

    def remote(src, dst, ssem, rsem, where):
        return pltpu.make_async_remote_copy(
            src_ref=src, dst_ref=dst, send_sem=ssem, recv_sem=rsem, device_id=where, device_id_type=MESH
        )

    loads = [
        pltpu.make_async_copy(a, b, load_sem.at[i])
        for i, (a, b) in enumerate(((x_hbm, x_v), (wq_hbm, wq), (wk_hbm, wk), (wv_hbm, wv), (wo_hbm, wo)))
    ]
    for copy in loads:
        copy.start()
    barrier = pltpu.get_barrier_semaphore()
    for s, t in everyone:
        pl.semaphore_signal(barrier, inc=1, device_id=dev(s, t), device_id_type=MESH)

    size = width // GROUPS
    chan = lax.broadcasted_iota(jnp.int32, (width, 128), 0)
    lane = lax.broadcasted_iota(jnp.int32, (width, 128), 1)
    gather = jnp.where((chan >= lane * size) & (chan < lane * size + size), 1.0, 0.0).astype(F32)
    chan_t = lax.broadcasted_iota(jnp.int32, (128, width), 1)
    lane_t = lax.broadcasted_iota(jnp.int32, (128, width), 0)
    spread = jnp.where((chan_t >= lane_t * size) & (chan_t < lane_t * size + size), 1.0, 0.0).astype(F32)

    def to_groups(row):
        return jnp.dot(
            jnp.broadcast_to(row, (8, width)), gather, preferred_element_type=F32, precision=lax.Precision.HIGHEST
        )[:1]

    def to_channels(row):
        return jnp.dot(
            jnp.broadcast_to(row, (8, 128)), spread, preferred_element_type=F32, precision=lax.Precision.HIGHEST
        )[:1]

    loads[0].wait()
    x = x_v[...].astype(F32)
    here = float(tok * size)
    mean_here = to_groups(jnp.sum(x, axis=0, keepdims=True)) / here
    off = x - to_channels(mean_here)
    dev_here = to_groups(jnp.sum(off * off, axis=0, keepdims=True))
    stat_own[...] = jnp.concatenate([mean_here, dev_here, jnp.zeros((6, 128), F32)], axis=0)
    pl.semaphore_wait(barrier, len(everyone))
    stats = []
    for s, t in everyone:
        i = s * nb + t
        copy = remote(stat_own, stat_in.at[i], st_send.at[i], st_recv.at[i], dev(s, t))
        copy.start()
        stats.append(copy)
    for copy in stats:
        copy.wait()
    means = [stat_own[0:1, :]] + [stat_in[s * nb + t, 0:1, :] for s, t in everyone]
    devs = [stat_own[1:2, :]] + [stat_in[s * nb + t, 1:2, :] for s, t in everyone]
    mean = sum(means) / float(na * nb)
    total_dev = sum(devs) + here * sum((m - mean) * (m - mean) for m in means)
    rstd = lax.rsqrt(total_dev / (here * na * nb) + 1e-05)
    mean_c = to_channels(mean)
    rstd_c = to_channels(rstd)
    normed = ((x_v[...].astype(F32) - mean_c) * rstd_c * gain_ref[...] + shift_ref[...]).astype(BF16)

    loads[1].wait()
    q = jnp.dot(normed, wq[...], preferred_element_type=F32) * (math.log2(math.e) / math.sqrt(HD))
    q = q.astype(BF16).astype(F32).T.astype(BF16)
    for g in range(na):
        q_own[g] = q[g * gw : (g + 1) * gw]
    q_copies = [
        remote(q_own.at[xor(me_a, s)], q_in.at[s - 1], q_send.at[s - 1], q_recv.at[s - 1], dev(s, 0))
        for s in range(1, na)
    ]
    for copy in q_copies:
        copy.start()
    loads[2].wait()
    k = jnp.dot(normed, wk[...], preferred_element_type=F32)
    k = k.astype(BF16).astype(F32).T.astype(BF16)
    for g in range(na):
        kv_own[g, 0:gw, :] = k[g * gw : (g + 1) * gw]
    loads[3].wait()
    v = jnp.dot(normed, wv[...], preferred_element_type=F32)
    for g in range(na):
        part = jnp.concatenate([v[:, g * gw : (g + 1) * gw], jnp.ones((tok, padw - gw), F32)], axis=1)
        kv_own[g, gw : gw + tok, :] = part.astype(BF16)
    z_copies = [
        remote(kv_own.at[xor(me_a, s)], kv.at[s, 0], z_send.at[s - 1], z_recv.at[s - 1], dev(s, 0))
        for s in range(1, na)
    ]
    for copy in z_copies:
        copy.start()
    own = pltpu.make_async_copy(kv_own.at[me_a], kv.at[0, 0], own_sem)
    own.start()

    def forward(s, t):
        src = kv.at[s, t - 1] if t % 2 and t > 1 else kv.at[s, 0]
        hop = 1 if t % 2 else t
        return remote(src, kv.at[s, t], f_send.at[s, t], f_recv.at[s, t], dev(0, hop))

    direct = [t for t in range(1, nb) if t == 1 or t % 2 == 0]
    relayed = [t for t in range(3, nb, 2)]

    def first(s):
        if s == 0:
            own.wait()
        else:
            z_copies[s - 1].wait()
        for t in reversed(direct):
            forward(s, t).start()

    def second(s):
        for t in relayed:
            forward(s, t - 1).wait_recv()
            forward(s, t).start()

    def third(s):
        for t in range(1, nb):
            if t + 1 not in relayed:
                forward(s, t).wait_recv()

    def unpack(i, block):
        for h in range(per):
            qh[h, i] = block[h * HD : (h + 1) * HD].astype(F32).T.astype(BF16)

    def compute(s, i, h):
        rows = pl.ds(pl.multiple_of(h * HD, HD), HD)
        query = qh[h, i]
        scores = [
            jnp.dot(query, kv[s, t, rows, :], preferred_element_type=F32) for t in range(nb)
        ]
        peak = functools.reduce(jnp.maximum, scores)
        peak = jnp.max(peak, axis=1, keepdims=True)
        if s:
            old = m_s[h, i][:, :1]
            peak = jnp.maximum(peak, old)
        mixed = None
        for t in range(nb):
            rounded = jnp.exp2(scores[t] - peak).astype(BF16)
            piece = jnp.dot(rounded, kv[s, t, gw : gw + tok, :], preferred_element_type=F32)
            mixed = piece if mixed is None else mixed + piece
        if s:
            mixed = acc[h, i] * jnp.exp2(old - peak) + mixed
        acc[h, i] = mixed
        if s < na - 1:
            m_s[h, i] = jnp.broadcast_to(peak, (tok, 128))

    def run(s, low, high):
        def step(j, c):
            compute(s, j // per, j % per)
            return c

        lax.fori_loop(low * per, high * per, step, 0)

    def finish(i):
        parts = []
        for h in range(per):
            a = acc[h, i]
            parts.append(a[:, h * HD : (h + 1) * HD] / a[:, gw : gw + 1])
        return jnp.concatenate(parts, axis=1).astype(BF16).astype(F32).T.astype(BF16)

    first(0)
    unpack(0, q_own[me_a])
    second(0)
    third(0)
    half = na // 2
    for s in range(na):
        if s == 0:
            run(0, 0, 1)
            for i in range(1, na):
                q_copies[i - 1].wait()
                unpack(i, q_in[i - 1])
            first(1)
            run(0, 1, half + 1)
            second(1)
            run(0, half + 1, na)
            third(1)
        elif s < na - 1:
            run(s, 0, half)
            first(s + 1)
            second(s + 1)
            run(s, half, na)
            third(s + 1)

    last = na - 1

    def back(j, c):
        i = last - j
        lax.fori_loop(0, per, lambda h, d: (compute(last, i, h), d)[1], 0)
        mix_out[i] = finish(i)
        remote(
            mix_out.at[i],
            mix_in.at[pl.ds(pl.multiple_of(me_a * gw, gw), gw)],
            o_send.at[i],
            o_recv.at[i],
            {ax_a: xor_traced(me_a, i, na), ax_b: me_b},
        ).start()
        return c

    lax.fori_loop(0, last, back, 0)
    lax.fori_loop(0, per, lambda h, d: (compute(last, 0, h), d)[1], 0)
    mix_in[pl.ds(pl.multiple_of(me_a * gw, gw), gw), :] = finish(0)
    loads[4].wait()
    for s in range(na):
        for t in range(1, nb):
            forward(s, t).wait_send()
    for i in range(1, na):
        copy = remote(
            mix_out.at[i],
            mix_in.at[pl.ds(pl.multiple_of(xor(me_a, i) * gw, gw), gw)],
            o_send.at[i],
            o_recv.at[i],
            dev(i, 0),
        )
        copy.wait()
    mixed = mix_in[...].astype(F32).T.astype(BF16)
    result = jnp.dot(mixed, wo[...], preferred_element_type=F32) + bias_ref[...]
    out_ref[...] = result.astype(BF16)


def local(sizes, latent, gain, shift, wq, wk, wv, wo, bias):
    rows, cols, width = latent.shape
    tok = rows * cols
    wide = wq.shape[1]
    heads = wide // HD
    ax_a, ax_b = ("row", "col") if heads % sizes["row"] == 0 else ("col", "row")
    na, nb = sizes[ax_a], sizes[ax_b]
    per = heads // na
    gw = per * HD
    padw = (gw // 128 + 1) * 128
    assert padw == tok
    vm = pltpu.VMEM
    dma = pltpu.SemaphoreType.DMA
    anyspec = pl.BlockSpec(memory_space=pl.ANY)
    vspec = pl.BlockSpec(memory_space=pltpu.VMEM)
    out = pl.pallas_call(
        functools.partial(kernel, ax_a, ax_b, na, nb, tok, width, heads, per),
        out_shape=jax.ShapeDtypeStruct((tok, width), BF16),
        in_specs=[anyspec, vspec, vspec, anyspec, anyspec, anyspec, anyspec, vspec],
        out_specs=vspec,
        scratch_shapes=[
            vm((tok, width), BF16),
            vm((width, wide), BF16),
            vm((width, wide), BF16),
            vm((width, wide), BF16),
            vm((wide, width), BF16),
            vm((8, 128), F32),
            vm((na * nb, 8, 128), F32),
            vm((na, gw, tok), BF16),
            vm((na - 1, gw, tok), BF16),
            vm((na, gw + tok, padw), BF16),
            vm((na, nb, gw + tok, padw), BF16),
            vm((per, na, tok, HD), BF16),
            vm((per, na, tok, 128), F32),
            vm((per, na, tok, padw), F32),
            vm((na, gw, tok), BF16),
            vm((wide, tok), BF16),
            dma((5,)),
            dma,
            dma((na * nb,)),
            dma((na * nb,)),
            dma((na - 1,)),
            dma((na - 1,)),
            dma((na - 1,)),
            dma((na - 1,)),
            dma((na, nb)),
            dma((na, nb)),
            dma((na,)),
            dma((na,)),
        ],
        compiler_params=pltpu.CompilerParams(
            collective_id=0, has_side_effects=True, vmem_limit_bytes=56 * 1024 * 1024
        ),
    )(
        latent.reshape(tok, width), gain.reshape(1, width), shift.reshape(1, width),
        wq, wk, wv, wo, bias.reshape(1, width),
    )
    return out.reshape(rows, cols, width)


def solution(mesh):
    placed = (P(("img", "row"), "col", None), P(), P(), P(), P(), P(), P(), P())
    return jax.shard_map(
        functools.partial(local, dict(mesh.shape)),
        mesh=mesh, in_specs=placed, out_specs=P(("img", "row"), "col", None), check_vma=False,
    )
```

time: 275 us -> 90.3 us (0.33)
  waiting for transfers between devices: 108 us -> 0 us
  Pallas kernels: 0 us -> 84 us
  blocking collectives: 64.4 us -> 0 us
  matrix products: 55.3 us -> 0 us
  between operations: 13.5 us -> 0.01 us
  other arithmetic: 13.1 us -> 0 us
  local copies, waits for them, and re-layouts: 18.5 us -> 5.83 us
    all_gather x2 -> x0, waiting for transfers between devices: 107 us -> none  [the longest x1 54 us: local(): lax.all_gather(keys, ('row', 'col'), axis=0, tiled=True)]
    pallas_call x0 -> x1, Pallas kernels: none -> 84 us  [local(): pl.pallas_call(functools.partial(kernel, ax_a, ax_b, na, nb, tok, width,...]
    psum x2 -> x0, blocking collectives: 64.4 us -> none  [the longest x1 34.9 us: local(): group_total = lax.psum(jnp.sum(grouped, axis=(0, 2)), ('row', 'col'))]
    dot_general x28 -> x0, matrix products: 55.3 us -> none  [the longest x12 22.8 us: per_head(): jnp.dot(rounded, value_one, preferred_element_type=jnp.float32)]
    all_gather x2 -> x0, local copies, waits for them, and re-layouts: 17.4 us -> none  [the longest x1 8.75 us: local(): lax.all_gather(values, ('row', 'col'), axis=0, tiled=True)]
    reduce_sum x16 -> x0, other arithmetic: 11.4 us -> none  [the longest x12 8.6 us: per_head(): total_new = total_old * factor + jnp.sum(weights, axis=1)]
    reshape x0 -> x3, local copies, waits for them, and re-layouts: none -> 3.86 us  [the longest x1 1.29 us: local(): bias.reshape(1, width)]
  transfers between devices with their start and end apart: 2 -> 0, of which waited for: 2 -> 0; matrix products, arithmetic and copies ran while one was open for 5% -> 0% of each run, Pallas kernels for 0% -> 0%
where the time goes in v1:
time: 90.3 us; the launch traced here: 89.9 us
  Pallas kernels  84 us (93%)
  local copies, waits for them, and re-layouts  5.83 us (6%)
    pallas_call x1, Pallas kernels, local(): pl.pallas_call(functools.partial(kernel, ax_a, ax_b, na, nb, tok, width,...  84 us
    unnamed x1, local copies, waits for them, and re-layouts  1.97 us

profile of v1, /device:TPU:0, one launch (start us, length us, event | category | flops | bytes accessed | tf_op | source)
XLA Modules:
  0.0 89.9 jit_solution(9580254097731502405)
XLA Ops:
  0.0 1.3 %reshape.16.gain_ref = f32[1,1280]{1,0:T(1,128)} reshape(f32[1280]{0:T(1024)} %param.9) | data formatting | bytes 10240 | tf_op jit(solution)/shard_map/reshape | solution.py:318
  1.3 1.3 %reshape.17.shift_ref = f32[1,1280]{1,0:T(1,128)} reshape(f32[1280]{0:T(1024)} %param.10) | data formatting | bytes 10240 | tf_op jit(solution)/shard_map/reshape | solution.py:318
  2.6 1.3 %reshape.18.bias_ref = f32[1,1280]{1,0:T(1,128)} reshape(f32[1280]{0:T(1024)} %param.15) | data formatting | bytes 10240 | tf_op jit(solution)/shard_map/reshape | solution.py:319
  3.9 84.0 %shard_map.82 = bf16[256,1280]{1,0:T(8,128)(2,1)} custom-call(bf16[256,1280]{1,0:T(8,128)(2,1)} %bitcast.3, f32[1,1280]{1,0:T(1,128)} %reshape.16.gain_ref, f32[1,1280]{1,0:T(1,128)} %reshape.17.shift_ref, bf16[1280,768]{1,0:T(8,128)(2,1)} %wq_hbm.1, bf16[1280,768]{1,0:T(8,128)(2,1)} %wk_hbm.1, bf16[1280,768]{1,0:T(8,128)(2,1)} %wv_hbm.1, ...), custom_call_target="tpu_custom_call" | custom-call | tf_op jit(solution)/shard_map/pallas_call | solution.py:279
  87.9 2.0 %copy.10 = bf16[16,16,1280]{2,1,0:T(8,128)(2,1)} copy(bf16[16,16,1280]{2,1,0:T(8,128)(2,1)} %bitcast.2) | data formatting | bytes 1310720

commit v2 on v1

--- a/solution.py
+++ b/solution.py
@@ -104,7 +104,7 @@
     rstd = lax.rsqrt(total_dev / (here * na * nb) + 1e-05)
     mean_c = to_channels(mean)
     rstd_c = to_channels(rstd)
-    normed = ((x_v[...].astype(F32) - mean_c) * rstd_c * gain_ref[...] + shift_ref[...]).astype(BF16)
+    normed = ((x_v[...].astype(F32) - mean_c) * rstd_c * gain_ref[...][None, :] + shift_ref[...][None, :]).astype(BF16)
 
     loads[1].wait()
     q = jnp.dot(normed, wq[...], preferred_element_type=F32) * (math.log2(math.e) / math.sqrt(HD))
@@ -166,12 +166,13 @@
         for h in range(per):
             qh[h, i] = block[h * HD : (h + 1) * HD].astype(F32).T.astype(BF16)
 
-    def compute(s, i, h):
-        rows = pl.ds(pl.multiple_of(h * HD, HD), HD)
+    def score(s, i, h):
         query = qh[h, i]
-        scores = [
-            jnp.dot(query, kv[s, t, rows, :], preferred_element_type=F32) for t in range(nb)
+        return [
+            jnp.dot(query, kv[s, t, h * HD : (h + 1) * HD, :], preferred_element_type=F32) for t in range(nb)
         ]
+
+    def absorb(s, i, h, scores):
         peak = functools.reduce(jnp.maximum, scores)
         peak = jnp.max(peak, axis=1, keepdims=True)
         if s:
@@ -188,12 +189,15 @@
         if s < na - 1:
             m_s[h, i] = jnp.broadcast_to(peak, (tok, 128))
 
+    def compute(s, i):
+        scores = score(s, i, 0)
+        for h in range(per):
+            later = score(s, i, h + 1) if h + 1 < per else None
+            absorb(s, i, h, scores)
+            scores = later
+
     def run(s, low, high):
-        def step(j, c):
-            compute(s, j // per, j % per)
-            return c
-
-        lax.fori_loop(low * per, high * per, step, 0)
+        lax.fori_loop(low, high, lambda i, c: (compute(s, i), c)[1], 0)
 
     def finish(i):
         parts = []
@@ -229,7 +233,7 @@
 
     def back(j, c):
         i = last - j
-        lax.fori_loop(0, per, lambda h, d: (compute(last, i, h), d)[1], 0)
+        compute(last, i)
         mix_out[i] = finish(i)
         remote(
             mix_out.at[i],
@@ -241,7 +245,7 @@
         return c
 
     lax.fori_loop(0, last, back, 0)
-    lax.fori_loop(0, per, lambda h, d: (compute(last, 0, h), d)[1], 0)
+    compute(last, 0)
     mix_in[pl.ds(pl.multiple_of(me_a * gw, gw), gw), :] = finish(0)
     loads[4].wait()
     for s in range(na):
@@ -257,7 +261,7 @@
         )
         copy.wait()
     mixed = mix_in[...].astype(F32).T.astype(BF16)
-    result = jnp.dot(mixed, wo[...], preferred_element_type=F32) + bias_ref[...]
+    result = jnp.dot(mixed, wo[...], preferred_element_type=F32) + bias_ref[...][None, :]
     out_ref[...] = result.astype(BF16)
 
 
@@ -315,8 +319,7 @@
             collective_id=0, has_side_effects=True, vmem_limit_bytes=56 * 1024 * 1024
         ),
     )(
-        latent.reshape(tok, width), gain.reshape(1, width), shift.reshape(1, width),
-        wq, wk, wv, wo, bias.reshape(1, width),
+        latent.reshape(tok, width), gain, shift, wq, wk, wv, wo, bias,
     )
     return out.reshape(rows, cols, width)
 

time: 90.3 us -> 76.5 us (0.85)
  Pallas kernels: 84 us -> 74.3 us
  local copies, waits for them, and re-layouts: 5.83 us -> 1.97 us
    pallas_call x1, Pallas kernels: 84 us -> 74.3 us  [local(): pl.pallas_call(functools.partial(kernel, ax_a, ax_b, na, nb, tok, width,...]
    reshape x3 -> x0, local copies, waits for them, and re-layouts: 3.86 us -> none  [the longest x1 1.29 us: local(): bias.reshape(1, width)]
where the time goes in v2:
time: 76.5 us; the launch traced here: 76.3 us
  Pallas kernels  74.3 us (97%)
  local copies, waits for them, and re-layouts  1.97 us (3%)
    pallas_call x1, Pallas kernels, local(): pl.pallas_call(functools.partial(kernel, ax_a, ax_b, na, nb, tok, width,...  74.3 us
    unnamed x1, local copies, waits for them, and re-layouts  1.97 us

profile of v2, /device:TPU:0, one launch (start us, length us, event | category | flops | bytes accessed | tf_op | source)
XLA Modules:
  0.0 76.3 jit_solution(4921615770220704907)
XLA Ops:
  0.0 74.3 %shard_map.82 = bf16[256,1280]{1,0:T(8,128)(2,1)} custom-call(bf16[256,1280]{1,0:T(8,128)(2,1)} %bitcast.3, f32[1280]{0:T(1024)} %gain_ref.1, f32[1280]{0:T(1024)} %shift_ref.1, bf16[1280,768]{1,0:T(8,128)(2,1)} %wq_hbm.1, bf16[1280,768]{1,0:T(8,128)(2,1)} %wk_hbm.1, bf16[1280,768]{1,0:T(8,128)(2,1)} %wv_hbm.1, bf16[768,1280]{1,0:T(8,128)(2,1)} %wo_hbm.1, ...), custom_call_target="tpu_custom_call" | custom-call | tf_op jit(solution)/shard_map/pallas_call | solution.py:283
  74.3 2.0 %copy.10 = bf16[16,16,1280]{2,1,0:T(8,128)(2,1)} copy(bf16[16,16,1280]{2,1,0:T(8,128)(2,1)} %bitcast.2) | data formatting | bytes 1310720

commit v3 on v2

--- a/solution.py
+++ b/solution.py
@@ -36,13 +36,14 @@
     ax_a, ax_b, na, nb, tok, width, wide_heads, per,
     x_hbm, gain_ref, shift_ref, wq_hbm, wk_hbm, wv_hbm, wo_hbm, bias_ref,
     out_ref,
-    x_v, wq, wk, wv, wo, stat_own, stat_in, q_own, q_in, kv_own, kv, qh, m_s, acc, mix_out, mix_in,
+    x_v, wq, wk, wv, wo, stat_own, stat_in, q_own, q_in, k_own, v_own, kbuf, vbuf, v_full, qh, m_s, acc, mix_out, mix_in,
     load_sem, own_sem, st_send, st_recv, q_send, q_recv, z_send, z_recv, f_send, f_recv, o_send, o_recv,
 ):
     me_a = lax.axis_index(ax_a)
     me_b = lax.axis_index(ax_b)
     gw = per * HD
-    padw = kv.shape[-1]
+    padw = v_full.shape[-1]
+    whole, half_tok = gw // 128, tok // 2
     everyone = [(s, t) for s in range(na) for t in range(nb) if s or t]
 
     def dev(s, t):
@@ -121,46 +122,66 @@
     k = jnp.dot(normed, wk[...], preferred_element_type=F32)
     k = k.astype(BF16).astype(F32).T.astype(BF16)
     for g in range(na):
-        kv_own[g, 0:gw, :] = k[g * gw : (g + 1) * gw]
+        k_own[g] = k[g * gw : (g + 1) * gw]
     loads[3].wait()
     v = jnp.dot(normed, wv[...], preferred_element_type=F32)
     for g in range(na):
-        part = jnp.concatenate([v[:, g * gw : (g + 1) * gw], jnp.ones((tok, padw - gw), F32)], axis=1)
-        kv_own[g, gw : gw + tok, :] = part.astype(BF16)
-    z_copies = [
-        remote(kv_own.at[xor(me_a, s)], kv.at[s, 0], z_send.at[s - 1], z_recv.at[s - 1], dev(s, 0))
-        for s in range(1, na)
-    ]
-    for copy in z_copies:
+        part = v[:, g * gw : (g + 1) * gw].astype(BF16).astype(F32)
+        for n in range(whole):
+            v_own[g, n * tok : (n + 1) * tok, :] = part[:, n * 128 : (n + 1) * 128].astype(BF16)
+        rest = part[:, whole * 128 :]
+        folded = jnp.concatenate([rest[:half_tok], rest[half_tok:]], axis=1)
+        v_own[g, whole * tok :, :] = folded.astype(BF16)
+    owned, landed = (k_own, v_own), (kbuf, vbuf)
+
+    def exchange(s, p):
+        return remote(
+            owned[p].at[xor(me_a, s)], landed[p].at[s, 0], z_send.at[s - 1, p], z_recv.at[s - 1, p], dev(s, 0)
+        )
+
+    for p in range(2):
+        for s in (3, 1):
+            exchange(s, p).start()
+    own = [pltpu.make_async_copy(owned[p].at[me_a], landed[p].at[0, 0], own_sem.at[p]) for p in range(2)]
+    for copy in own:
         copy.start()
-    own = pltpu.make_async_copy(kv_own.at[me_a], kv.at[0, 0], own_sem)
-    own.start()
-
-    def forward(s, t):
-        src = kv.at[s, t - 1] if t % 2 and t > 1 else kv.at[s, 0]
+
+    def forward(s, t, p):
+        buf = landed[p]
+        src = buf.at[s, t - 1] if t % 2 and t > 1 else buf.at[s, 0]
         hop = 1 if t % 2 else t
-        return remote(src, kv.at[s, t], f_send.at[s, t], f_recv.at[s, t], dev(0, hop))
+        return remote(src, buf.at[s, t], f_send.at[s, t, p], f_recv.at[s, t, p], dev(0, hop))
 
     direct = [t for t in range(1, nb) if t == 1 or t % 2 == 0]
     relayed = [t for t in range(3, nb, 2)]
 
     def first(s):
-        if s == 0:
-            own.wait()
-        else:
-            z_copies[s - 1].wait()
-        for t in reversed(direct):
-            forward(s, t).start()
+        for p in range(2):
+            if s == 0:
+                own[p].wait()
+            else:
+                exchange(s, p).wait_recv()
+            for t in reversed(direct):
+                forward(s, t, p).start()
 
     def second(s):
-        for t in relayed:
-            forward(s, t - 1).wait_recv()
-            forward(s, t).start()
+        for p in range(2):
+            for t in relayed:
+                forward(s, t - 1, p).wait_recv()
+                forward(s, t, p).start()
 
     def third(s):
-        for t in range(1, nb):
-            if t + 1 not in relayed:
-                forward(s, t).wait_recv()
+        for t in range(nb):
+            for p in range(2):
+                if t and t + 1 not in relayed:
+                    forward(s, t, p).wait_recv()
+            for n in range(whole):
+                v_full[t, :, n * 128 : (n + 1) * 128] = vbuf[s, t, n * tok : (n + 1) * tok, :]
+            folded = vbuf[s, t, whole * tok :, :].astype(F32)
+            lower = jnp.concatenate([folded[:, :HD], jnp.ones((half_tok, 128 - HD), F32)], axis=1)
+            upper = jnp.concatenate([folded[:, HD:], jnp.ones((half_tok, 128 - HD), F32)], axis=1)
+            v_full[t, :half_tok, whole * 128 :] = lower.astype(BF16)
+            v_full[t, half_tok:, whole * 128 :] = upper.astype(BF16)
 
     def unpack(i, block):
         for h in range(per):
@@ -169,7 +190,7 @@
     def score(s, i, h):
         query = qh[h, i]
         return [
-            jnp.dot(query, kv[s, t, h * HD : (h + 1) * HD, :], preferred_element_type=F32) for t in range(nb)
+            jnp.dot(query, kbuf[s, t, h * HD : (h + 1) * HD, :], preferred_element_type=F32) for t in range(nb)
         ]
 
     def absorb(s, i, h, scores):
@@ -181,12 +202,12 @@
         mixed = None
         for t in range(nb):
             rounded = jnp.exp2(scores[t] - peak).astype(BF16)
-            piece = jnp.dot(rounded, kv[s, t, gw : gw + tok, :], preferred_element_type=F32)
+            piece = jnp.dot(rounded, v_full[t], preferred_element_type=F32)
             mixed = piece if mixed is None else mixed + piece
         if s:
             mixed = acc[h, i] * jnp.exp2(old - peak) + mixed
         acc[h, i] = mixed
-        if s < na - 1:
+        if s != last:
             m_s[h, i] = jnp.broadcast_to(peak, (tok, 128))
 
     def compute(s, i):
@@ -206,33 +227,35 @@
             parts.append(a[:, h * HD : (h + 1) * HD] / a[:, gw : gw + 1])
         return jnp.concatenate(parts, axis=1).astype(BF16).astype(F32).T.astype(BF16)
 
+    last = 2
     first(0)
     unpack(0, q_own[me_a])
     second(0)
     third(0)
-    half = na // 2
-    for s in range(na):
-        if s == 0:
-            run(0, 0, 1)
-            for i in range(1, na):
-                q_copies[i - 1].wait()
-                unpack(i, q_in[i - 1])
-            first(1)
-            run(0, 1, half + 1)
-            second(1)
-            run(0, half + 1, na)
-            third(1)
-        elif s < na - 1:
-            run(s, 0, half)
-            first(s + 1)
-            second(s + 1)
-            run(s, half, na)
-            third(s + 1)
-
-    last = na - 1
+    run(0, 0, 1)
+    for i in range(1, na):
+        q_copies[i - 1].wait()
+        unpack(i, q_in[i - 1])
+    run(0, 1, 2)
+    first(1)
+    run(0, 2, 3)
+    first(3)
+    for p in range(2):
+        exchange(2, p).start()
+    second(1)
+    run(0, 3, 4)
+    second(3)
+    third(1)
+    run(1, 0, 4)
+    first(2)
+    third(3)
+    run(3, 0, 2)
+    second(2)
+    run(3, 2, 4)
+    third(2)
 
     def back(j, c):
-        i = last - j
+        i = na - 1 - j
         compute(last, i)
         mix_out[i] = finish(i)
         remote(
@@ -244,13 +267,16 @@
         ).start()
         return c
 
-    lax.fori_loop(0, last, back, 0)
+    lax.fori_loop(0, na - 1, back, 0)
     compute(last, 0)
     mix_in[pl.ds(pl.multiple_of(me_a * gw, gw), gw), :] = finish(0)
     loads[4].wait()
-    for s in range(na):
-        for t in range(1, nb):
-            forward(s, t).wait_send()
+    for p in range(2):
+        for s in range(na):
+            if s:
+                exchange(s, p).wait_send()
+            for t in range(1, nb):
+                forward(s, t, p).wait_send()
     for i in range(1, na):
         copy = remote(
             mix_out.at[i],
@@ -275,7 +301,8 @@
     per = heads // na
     gw = per * HD
     padw = (gw // 128 + 1) * 128
-    assert padw == tok
+    assert na == 4 and gw % 128 == HD
+    vrows = tok * (gw // 128) + tok // 2
     vm = pltpu.VMEM
     dma = pltpu.SemaphoreType.DMA
     anyspec = pl.BlockSpec(memory_space=pl.ANY)
@@ -295,23 +322,26 @@
             vm((na * nb, 8, 128), F32),
             vm((na, gw, tok), BF16),
             vm((na - 1, gw, tok), BF16),
-            vm((na, gw + tok, padw), BF16),
-            vm((na, nb, gw + tok, padw), BF16),
+            vm((na, gw, tok), BF16),
+            vm((na, vrows, 128), BF16),
+            vm((na, nb, gw, tok), BF16),
+            vm((na, nb, vrows, 128), BF16),
+            vm((nb, tok, padw), BF16),
             vm((per, na, tok, HD), BF16),
             vm((per, na, tok, 128), F32),
             vm((per, na, tok, padw), F32),
             vm((na, gw, tok), BF16),
             vm((wide, tok), BF16),
             dma((5,)),
-            dma,
+            dma((2,)),
             dma((na * nb,)),
             dma((na * nb,)),
             dma((na - 1,)),
             dma((na - 1,)),
-            dma((na - 1,)),
-            dma((na - 1,)),
-            dma((na, nb)),
-            dma((na, nb)),
+            dma((na - 1, 2)),
+            dma((na - 1, 2)),
+            dma((na, nb, 2)),
+            dma((na, nb, 2)),
             dma((na,)),
             dma((na,)),
         ],

time: 76.5 us -> 66.6 us (0.87)
  Pallas kernels: 74.3 us -> 64.4 us
    pallas_call x1, Pallas kernels: 74.3 us -> 64.4 us  [local(): pl.pallas_call(functools.partial(kernel, ax_a, ax_b, na, nb, tok, width,...]
where the time goes in v3:
time: 66.6 us; the launch traced here: 66.4 us
  Pallas kernels  64.4 us (97%)
  local copies, waits for them, and re-layouts  1.97 us (3%)
    pallas_call x1, Pallas kernels, local(): pl.pallas_call(functools.partial(kernel, ax_a, ax_b, na, nb, tok, width,...  64.4 us
    unnamed x1, local copies, waits for them, and re-layouts  1.97 us

profile of v3, /device:TPU:0, one launch (start us, length us, event | category | flops | bytes accessed | tf_op | source)
XLA Modules:
  0.0 66.4 jit_solution(2739838012211336542)
XLA Ops:
  0.0 64.4 %shard_map.82 = bf16[256,1280]{1,0:T(8,128)(2,1)} custom-call(bf16[256,1280]{1,0:T(8,128)(2,1)} %bitcast.3, f32[1280]{0:T(1024)} %gain_ref.1, f32[1280]{0:T(1024)} %shift_ref.1, bf16[1280,768]{1,0:T(8,128)(2,1)} %wq_hbm.1, bf16[1280,768]{1,0:T(8,128)(2,1)} %wk_hbm.1, bf16[1280,768]{1,0:T(8,128)(2,1)} %wv_hbm.1, bf16[768,1280]{1,0:T(8,128)(2,1)} %wo_hbm.1, ...), custom_call_target="tpu_custom_call" | custom-call | tf_op jit(solution)/shard_map/pallas_call | solution.py:310
  64.4 2.0 %copy.10 = bf16[16,16,1280]{2,1,0:T(8,128)(2,1)} copy(bf16[16,16,1280]{2,1,0:T(8,128)(2,1)} %bitcast.2) | data formatting | bytes 1310720

commit v4 on v3

--- a/solution.py
+++ b/solution.py
@@ -103,8 +103,11 @@
     mean = sum(means) / float(na * nb)
     total_dev = sum(devs) + here * sum((m - mean) * (m - mean) for m in means)
     rstd = lax.rsqrt(total_dev / (here * na * nb) + 1e-05)
-    mean_c = to_channels(mean)
-    rstd_c = to_channels(rstd)
+    both = jnp.dot(
+        jnp.concatenate([mean, rstd, jnp.zeros((6, 128), F32)], axis=0), spread,
+        preferred_element_type=F32, precision=lax.Precision.HIGHEST,
+    )
+    mean_c, rstd_c = both[0:1], both[1:2]
     normed = ((x_v[...].astype(F32) - mean_c) * rstd_c * gain_ref[...][None, :] + shift_ref[...][None, :]).astype(BF16)
 
     loads[1].wait()
@@ -116,7 +119,7 @@
         remote(q_own.at[xor(me_a, s)], q_in.at[s - 1], q_send.at[s - 1], q_recv.at[s - 1], dev(s, 0))
         for s in range(1, na)
     ]
-    for copy in q_copies:
+    for copy in reversed(q_copies):
         copy.start()
     loads[2].wait()
     k = jnp.dot(normed, wk[...], preferred_element_type=F32)

time: 66.6 us -> 66.3 us (level)
  no operation moved by 1% of the time
where the time goes in v4:
time: 66.3 us; the launch traced here: 66.1 us
  Pallas kernels  64.1 us (97%)
  local copies, waits for them, and re-layouts  1.97 us (3%)
    pallas_call x1, Pallas kernels, local(): pl.pallas_call(functools.partial(kernel, ax_a, ax_b, na, nb, tok, width,...  64.1 us
    unnamed x1, local copies, waits for them, and re-layouts  1.97 us

profile of v4, /device:TPU:0, one launch (start us, length us, event | category | flops | bytes accessed | tf_op | source)
XLA Modules:
  0.0 66.1 jit_solution(16871175027877671080)
XLA Ops:
  0.0 64.1 %shard_map.82 = bf16[256,1280]{1,0:T(8,128)(2,1)} custom-call(bf16[256,1280]{1,0:T(8,128)(2,1)} %bitcast.3, f32[1280]{0:T(1024)} %gain_ref.1, f32[1280]{0:T(1024)} %shift_ref.1, bf16[1280,768]{1,0:T(8,128)(2,1)} %wq_hbm.1, bf16[1280,768]{1,0:T(8,128)(2,1)} %wk_hbm.1, bf16[1280,768]{1,0:T(8,128)(2,1)} %wv_hbm.1, bf16[768,1280]{1,0:T(8,128)(2,1)} %wo_hbm.1, ...), custom_call_target="tpu_custom_call" | custom-call | tf_op jit(solution)/shard_map/pallas_call | solution.py:313
  64.1 2.0 %copy.10 = bf16[16,16,1280]{2,1,0:T(8,128)(2,1)} copy(bf16[16,16,1280]{2,1,0:T(8,128)(2,1)} %bitcast.2) | data formatting | bytes 1310720
